TPU v7x, 32 devices: a whole 2x2x4 slice. The times are simulated.
32 devices in a mesh: gx: 16 (over z, y, core), gz: 2 (over x).
Axes of the slice: x: 2, y: 2, z: 4, core: 2. Of those that a mesh axis runs over, the one named last changes fastest.
Arguments:
- populations: float32 [19, 32, 16, 256], P(None, 'gx', None, 'gz'), as said below
- solid: int32 [32, 16, 256], P('gx', None, 'gz'), may hold values 0 or 1
- cell_index: int32 [65536], P(('gx', 'gz')), may hold values from 0 to 4095
- offset: float32 [65536], P(('gx', 'gz')), may hold values from 0 to 1
- velocity: float32 [3, 65536], P(None, ('gx', 'gz')), may hold values from -0.6 to 0.6
- mass: float32 [65536], P(('gx', 'gz')), may hold values from 0.2 to 2
- counts: int32 [16, 2], P('gx', 'gz'), may hold values from 512 to 2048, as said below
Outputs:
- new_populations: float32 [19, 32, 16, 256], P(None, 'gx', None, 'gz')
- new_velocity: float32 [3, 65536], P(None, ('gx', 'gz'))
Inputs may be any that keep to these rules, and one draw needn't show every extreme that they name: `cell_index`: an index of a cell of the device's own block, numbered with z fastest, then y, then x. `counts`: some device has all 2048 slots live in every draw. Positive populations.
All inputs are finite; a program needn't handle non-finite values. No bound on the sum of `solid` on one device may be relied on, other than what follows from the above.
Results may differ from a plain program's by a relative error of at most 0.0001.
Values sent between devices are 32-bit elements; how exact they have to be, the bound alone decides.
A program may use at most 64 MiB of HBM per device.

v0:
```python
import jax
import jax.numpy as jnp
import numpy as np
from jax import lax
from jax.sharding import PartitionSpec as P

SUBSTEPS = 2


LATTICE = np.array(
    [
        [0, 0, 0],
        [1, 0, 0],
        [-1, 0, 0],
        [0, 1, 0],
        [0, -1, 0],
        [0, 0, 1],
        [0, 0, -1],
        [1, 1, 0],
        [-1, -1, 0],
        [1, -1, 0],
        [-1, 1, 0],
        [1, 0, 1],
        [-1, 0, -1],
        [1, 0, -1],
        [-1, 0, 1],
        [0, 1, 1],
        [0, -1, -1],
        [0, 1, -1],
        [0, -1, 1],
    ]
)
WEIGHTS = [1.0 / 3.0] + [1.0 / 18.0] * 6 + [1.0 / 36.0] * 12
OPPOSITE = [int(np.where((LATTICE == -LATTICE[k]).all(1))[0][0]) for k in range(19)]
relax_time = 0.6
coupling = 0.5
settle = 0.02
body_force = 0.0001


def extended_2(value, sides, width):
    for axis, dim in sides:
        count, length = (lax.axis_size(axis), value.shape[dim])
        up = [(i, (i + 1) % count) for i in range(count)]
        down = [(j, i) for i, j in up]
        last = lax.slice_in_dim(value, length - width, length, axis=dim)
        leading = lax.slice_in_dim(value, 0, width, axis=dim)
        before = lax.ppermute(last, axis, up)
        after = lax.ppermute(leading, axis, down)
        value = jnp.concatenate([before, value, after], axis=dim)
    return value


def shifted(block, axis, distance):
    devices = range(lax.axis_size(axis))
    route = [((i - distance) % len(devices), i) for i in devices]
    return lax.ppermute(block, axis, route)


def momenta(field):
    out = []
    for axis_id in range(3):
        total = jnp.zeros(field.shape[1:], jnp.float32)
        for index in range(19):
            if LATTICE[index, axis_id] != 0:
                total = total + float(LATTICE[index, axis_id]) * field[index]
        out.append(total)
    return out


def collide(field, force, solid):
    density = jnp.sum(field, axis=0)
    moment = momenta(field)
    flow = [(moment[d] + relax_time * force[d]) / density for d in range(3)]
    usq = flow[0] * flow[0] + flow[1] * flow[1] + flow[2] * flow[2]
    posts = []
    for index in range(19):
        along = jnp.zeros_like(density)
        for d in range(3):
            if LATTICE[index, d] != 0:
                along = along + float(LATTICE[index, d]) * flow[d]
        feq = WEIGHTS[index] * density * (1.0 + 3.0 * along + 4.5 * along * along - 1.5 * usq)
        posts.append(field[index] - (field[index] - feq) / relax_time)
    post = jnp.stack(posts)
    return jnp.where(solid[None] > 0, field[jnp.array(OPPOSITE)], post)


def extend(post):
    return extended_2(post, (("gx", 1), ("gz", 3)), 1)


def stream(padded, depth_x, depth_z):
    rows = []
    for index in range(19):
        start_x = 1 - int(LATTICE[index, 0])
        start_z = 1 - int(LATTICE[index, 2])
        piece = padded[index, start_x : start_x + depth_x, :, start_z : start_z + depth_z]
        rows.append(jnp.roll(piece, int(LATTICE[index, 1]), axis=1))
    return jnp.stack(rows)


def body(populations, solid, cell_index, offset, velocity, mass, counts):
    depth_x, ny_cells, depth_z = populations.shape[1:]
    plane = ny_cells * depth_z
    density = jnp.sum(populations, axis=0)
    cell_velocity = jnp.stack([m / density for m in momenta(populations)])
    front = shifted(cell_velocity[:, :1], "gx", -1)
    extended = jnp.concatenate([cell_velocity, front], axis=1).reshape(3, -1)
    slots = cell_index.shape[0]
    live = (jnp.arange(slots, dtype=jnp.int32) < counts.reshape(())).astype(jnp.float32)
    here = jnp.take(extended, cell_index, axis=1)
    ahead = jnp.take(extended, cell_index + plane, axis=1)
    particle_flow = (1.0 - offset) * here + offset * ahead
    change = coupling * live * (particle_flow - velocity)
    new_velocity = (velocity + change).at[1].add(-settle * live)
    push = -mass * change
    deposit = jnp.zeros((3, (depth_x + 1) * plane), jnp.float32)
    deposit = deposit.at[:, cell_index].add(push * (1.0 - offset))
    deposit = deposit.at[:, cell_index + plane].add(push * offset)
    deposit = deposit.reshape(3, depth_x + 1, ny_cells, depth_z)
    spill = shifted(deposit[:, depth_x:], "gx", 1)
    force = deposit[:, :depth_x].at[:, :1].add(spill)
    force = force.at[0].add(body_force)
    field = populations
    for step in range(SUBSTEPS):
        post = collide(field, force, solid)
        field = stream(extend(post), depth_x, depth_z)
    return (field, new_velocity)


def solution(mesh):
    return jax.shard_map(
        body,
        mesh=mesh,
        in_specs=(
            P(None, "gx", None, "gz"),
            P("gx", None, "gz"),
            P(("gx", "gz")),
            P(("gx", "gz")),
            P(None, ("gx", "gz")),
            P(("gx", "gz")),
            P("gx", "gz"),
        ),
        out_specs=(P(None, "gx", None, "gz"), P(None, ("gx", "gz"))),
        check_vma=False,
    )
```

profile of v0, /device:TPU:0, one launch (start us, length us, event | category | flops | bytes accessed | tf_op | source)
XLA Modules:
  0.0 108.2 jit_solution(7058924183126384428)
XLA Ops:
  0.6 1.0 reduce_sum.415
  1.6 0.9 bitcast_divide_fusion.5
  2.5 0.9 bitcast_divide_fusion.4
  3.4 0.9 bitcast_divide_fusion.3
  4.3 5.5 %collective-permute-start = (f32[3,1,16,128]{3,2,1,0:T(8,128)S(1)}, f32[3,1,16,128]{3,2,1,0:T(8,128)S(1)}, u32[]{:S(2)}, u32[]{:S(2)}) collective-permute-start(f32[3,1,16,128]{3,2,1,0:T(8,128)S(1)} %pad_maximum_fusion.3), channel_id=1, source_target_pairs={{2,0},{4,2},{6,4},{8,6},{10,8},{12,10},{14,12},{16,14},{18,16},{20... | collective-permute-start | bytes 73736 | tf_op jit(solution)/shard_map/ppermute | solution.py:57
  9.8 1.3 %compare_select_fusion.1 = (s32[2048]{0:T(1024)}, s32[2048]{0:T(1024)S(1)}, s32[2048]{0:T(1024)S(1)}, s32[2048]{0:T(1024)}) fusion(s32[2048]{0:T(1024)} %param.19), kind=kLoop, calls=%fused_computation.97 | loop fusion | flops 22528 | bytes 40960 | tf_op jit(solution)/shard_map/select_n | solution.py:119
  11.8 1.3 %broadcast_compare_fusion = pred[2,16,128]{2,1,0:T(8,128)(4,1)} fusion(s32[2,16,128]{2,1,0:T(8,128)} %param.18), kind=kLoop, calls=%fused_computation.416 | loop fusion | flops 4096 | bytes 20480 | tf_op jit(solution)/shard_map/gt | solution.py:85
  15.2 1.1 copy.761
  16.3 7.6 %gather_fusion.2 = f32[2048,3]{1,0:T(8,128)} fusion(f32[3,6144]{0,1:T(8,128)S(1)} %bitcast.301, s32[2048]{0:T(1024)S(1)} %get-tuple-element.170), kind=kCustom, calls=%fused_computation.clone | custom fusion | bytes 57344 | tf_op jit(solution)/shard_map/jit(_take)/gather | solution.py:111
  23.9 1.6 %copy.736 = f32[2048,3]{0,1:T(4,128)S(1)} copy(f32[2048,3]{1,0:T(8,128)} %gather_fusion.2) | data formatting | bytes 49152 | tf_op jit(solution)/shard_map/jit(_take)/gather | solution.py:111
  25.4 7.6 %gather_fusion.3 = f32[2048,3]{1,0:T(8,128)} fusion(f32[3,6144]{0,1:T(8,128)S(1)} %bitcast.302, s32[2048]{0:T(1024)S(1)} %get-tuple-element.171), kind=kCustom, calls=%fused_computation.1.clone | custom fusion | bytes 57344 | tf_op jit(solution)/shard_map/jit(_take)/gather | solution.py:112
  33.0 1.6 %copy.738 = f32[2048,3]{0,1:T(4,128)S(1)} copy(f32[2048,3]{1,0:T(8,128)} %gather_fusion.3) | data formatting | bytes 49152 | tf_op jit(solution)/shard_map/jit(_take)/gather | solution.py:112
  34.6 1.4 %copy.739 = f32[2048,3]{1,0:T(8,128)} copy(f32[2048,3]{0,1:T(4,128)S(1)} %get-tuple-element.112) | data formatting | bytes 49152 | tf_op jit(solution)/shard_map/mul | solution.py:118
  36.0 1.3 %copy.740 = f32[2048,3]{1,0:T(8,128)} copy(f32[2048,3]{0,1:T(4,128)S(1)} %get-tuple-element.111) | data formatting | bytes 49152 | tf_op jit(solution)/shard_map/mul | solution.py:119
  37.4 12.6 %scatter_custom_fusion = f32[3,6144]{0,1:T(8,128)S(1)} fusion(s32[2048]{0:T(1024)} %get-tuple-element.172, f32[2048,3]{1,0:T(8,128)} %copy.739, f32[]{:T(128)} %constant.166.clone.1), kind=kCustom, calls=%fused_computation.6 | custom fusion | flops 6144 | bytes 74240 | tf_op jit(solution)/shard_map/scatter-add | solution.py:118
  50.0 13.0 %scatter_fusion = f32[3,6144]{0,1:T(8,128)S(1)} fusion(f32[3,6144]{0,1:T(8,128)S(1)} %scatter_custom_fusion, s32[2048]{0:T(1024)} %get-tuple-element.169, f32[2048,3]{1,0:T(8,128)} %copy.740), kind=kCustom, calls=%fused_computation.5 | custom fusion | flops 6144 | bytes 81920 | tf_op jit(solution)/shard_map/scatter-add | solution.py:119
  63.0 1.4 %fusion.203 = (f32[3,1,16,128]{0,3,2,1:T(8,128)}, f32[3,1,16,128]{0,3,2,1:T(8,128)}) fusion(f32[3,3,16,128]{0,3,2,1:T(8,128)S(1)} %bitcast.299), kind=kLoop, calls=%fused_computation.445 | loop fusion | bytes 98304 | tf_op jit(solution)/shard_map/slice | solution.py:121
  64.4 2.2 %copy.765 = f32[3,1,16,128]{3,2,1,0:T(8,128)} copy(f32[3,1,16,128]{0,3,2,1:T(8,128)} %get-tuple-element.72) | data formatting | bytes 49152
  66.6 1.2 %pad_clamp_fusion = s32[1024]{0:T(1024)} fusion(s32[19]{0:T(128)} %constant.194), kind=kLoop, calls=%fused_computation.422 | loop fusion | flops 1024 | bytes 4172 | tf_op jit(solution)/shard_map/gather | solution.py:85
  67.8 1.4 %gather_fusion = f32[19,2,16,128]{3,2,1,0:T(8,128)} fusion(f32[19,2,16,128]{3,2,1,0:T(8,128)S(1)} %copy-done, s32[1024]{0:T(1024)} %pad_clamp_fusion), kind=kCustom, calls=%fused_computation.2 | custom fusion | bytes 622668 | tf_op jit(solution)/shard_map/gather | solution.py:85
  69.2 1.5 %slice.644 = f32[3,2,16,128]{0,3,2,1:T(8,128)} slice(f32[3,3,16,128]{0,3,2,1:T(8,128)S(1)} %bitcast.300), slice={[0:3], [0:2], [0:16], [0:128]} | slice | bytes 98304 | tf_op jit(solution)/shard_map/slice | solution.py:122
  70.7 2.3 %copy.763 = f32[3,2,16,128]{3,2,1,0:T(8,128)S(1)} copy(f32[3,2,16,128]{0,3,2,1:T(8,128)} %slice.644) | data formatting | bytes 98304
  73.0 1.6 %copy.764 = f32[3,1,16,128]{3,2,1,0:T(8,128)S(1)} copy(f32[3,1,16,128]{0,3,2,1:T(8,128)} %get-tuple-element.73) | data formatting | bytes 49152
  75.9 4.5 %collective-permute-start.3 = (f32[19,1,16,128]{3,2,1,0:T(8,128)S(1)}, f32[19,1,16,128]{3,2,1,0:T(8,128)S(1)}, u32[]{:S(2)}, u32[]{:S(2)}) collective-permute-start(f32[19,1,16,128]{3,2,1,0:T(8,128)S(1)} %get-tuple-element.110), channel_id=1, source_target_pairs={{2,0},{4,2},{6,4},{8,6},{10,8},{12,10},{14,12},{16,14},{18,16},{20... | collective-permute-start | bytes 466952 | tf_op jit(solution)/shard_map/ppermute | solution.py:49
  80.6 2.7 %collective-permute-done.2 = f32[19,1,16,128]{3,2,1,0:T(8,128)S(1)} collective-permute-done((f32[19,1,16,128]{3,2,1,0:T(8,128)S(1)}, f32[19,1,16,128]{3,2,1,0:T(8,128)S(1)}, u32[]{:S(2)}, u32[]{:S(2)}) %collective-permute-start.2) | collective-permute-done | bytes 155680 | tf_op jit(solution)/shard_map/ppermute | solution.py:48
  84.2 1.5 %collective-permute-start.4 = (f32[19,4,16,1]{0,2,3,1:T(8,128)S(1)}, f32[19,4,16,1]{0,2,3,1:T(8,128)S(1)}, u32[]{:S(2)}, u32[]{:S(2)}) collective-permute-start(f32[19,4,16,1]{0,2,3,1:T(8,128)S(1)} %copy.742), channel_id=1, source_target_pairs={{0,1},{1,0},{2,3},{3,2},{4,5},{5,4},{6,7},{7,6},{8,9},{9,8},{10,11... | collective-permute-start | bytes 14600 | tf_op jit(solution)/shard_map/ppermute | solution.py:48
  86.8 1.3 %collective-permute-done.4 = f32[19,4,16,1]{0,2,3,1:T(8,128)S(1)} collective-permute-done((f32[19,4,16,1]{0,2,3,1:T(8,128)S(1)}, f32[19,4,16,1]{0,2,3,1:T(8,128)S(1)}, u32[]{:S(2)}, u32[]{:S(2)}) %collective-permute-start.4) | collective-permute-done | bytes 4896 | tf_op jit(solution)/shard_map/ppermute | solution.py:48
  88.9 1.3 %collective-permute-done.5 = f32[19,4,16,1]{0,2,3,1:T(8,128)S(1)} collective-permute-done((f32[19,4,16,1]{0,2,3,1:T(8,128)S(1)}, f32[19,4,16,1]{0,2,3,1:T(8,128)S(1)}, u32[]{:S(2)}, u32[]{:S(2)}) %collective-permute-start.5) | collective-permute-done | bytes 4896 | tf_op jit(solution)/shard_map/ppermute | solution.py:49
  92.8 4.4 %collective-permute-start.7 = (f32[19,1,16,128]{3,2,1,0:T(8,128)S(1)}, f32[19,1,16,128]{3,2,1,0:T(8,128)S(1)}, u32[]{:S(2)}, u32[]{:S(2)}) collective-permute-start(f32[19,1,16,128]{3,2,1,0:T(8,128)S(1)} %get-tuple-element.101), channel_id=1, source_target_pairs={{2,0},{4,2},{6,4},{8,6},{10,8},{12,10},{14,12},{16,14},{18,16},{20... | collective-permute-start | bytes 466952 | tf_op jit(solution)/shard_map/ppermute | solution.py:49
  97.2 2.9 %collective-permute-done.6 = f32[19,1,16,128]{3,2,1,0:T(8,128)S(1)} collective-permute-done((f32[19,1,16,128]{3,2,1,0:T(8,128)S(1)}, f32[19,1,16,128]{3,2,1,0:T(8,128)S(1)}, u32[]{:S(2)}, u32[]{:S(2)}) %collective-permute-start.6) | collective-permute-done | bytes 155680 | tf_op jit(solution)/shard_map/ppermute | solution.py:48
  102.1 1.5 %collective-permute-start.9 = (f32[19,4,16,1]{0,2,3,1:T(8,128)S(1)}, f32[19,4,16,1]{0,2,3,1:T(8,128)S(1)}, u32[]{:S(2)}, u32[]{:S(2)}) collective-permute-start(f32[19,4,16,1]{0,2,3,1:T(8,128)S(1)} %copy.759), channel_id=1, source_target_pairs={{1,0},{0,1},{3,2},{2,3},{5,4},{4,5},{7,6},{6,7},{9,8},{8,9},{11,10... | collective-permute-start | bytes 14600 | tf_op jit(solution)/shard_map/ppermute | solution.py:49
  103.6 1.3 %collective-permute-done.8 = f32[19,4,16,1]{0,2,3,1:T(8,128)S(1)} collective-permute-done((f32[19,4,16,1]{0,2,3,1:T(8,128)S(1)}, f32[19,4,16,1]{0,2,3,1:T(8,128)S(1)}, u32[]{:S(2)}, u32[]{:S(2)}) %collective-permute-start.8) | collective-permute-done | bytes 4896 | tf_op jit(solution)/shard_map/ppermute | solution.py:48
  (155 shorter events, 13.6 us)
Async XLA Ops:
  4.3 30.3 %copy-start.2 = (f32[2048]{0:T(1024)S(1)}, f32[2048]{0:T(1024)}, u32[]{:S(2)}) copy-start(f32[2048]{0:T(1024)} %param.20) | copy-start | bytes 24580
  4.3 30.3 %copy-start.5 = (f32[3,2048]{1,0:T(4,128)S(1)}, f32[3,2048]{1,0:T(4,128)}, u32[]{:S(2)}) copy-start(f32[3,2048]{1,0:T(4,128)} %param.21) | copy-start | bytes 73732
  4.3 10.9 %collective-permute-start = (f32[3,1,16,128]{3,2,1,0:T(8,128)S(1)}, f32[3,1,16,128]{3,2,1,0:T(8,128)S(1)}, u32[]{:S(2)}, u32[]{:S(2)}) collective-permute-start(f32[3,1,16,128]{3,2,1,0:T(8,128)S(1)} %pad_maximum_fusion.3), channel_id=1, source_target_pairs={{2,0},{4,2},{6,4},{8,6},{10,8},{12,10},{14,12},{16,14},{18,16},{20... | collective-permute-start | bytes 73736 | tf_op jit(solution)/shard_map/ppermute | solution.py:57
  50.0 17.9 %copy-start = (f32[19,2,16,128]{3,2,1,0:T(8,128)S(1)}, f32[19,2,16,128]{3,2,1,0:T(8,128)}, u32[]{:S(2)}) copy-start(f32[19,2,16,128]{3,2,1,0:T(8,128)} %param.17) | copy-start | bytes 933892
  66.6 8.0 %collective-permute-start.1 = (f32[3,1,16,128]{3,2,1,0:T(8,128)}, f32[3,1,16,128]{3,2,1,0:T(8,128)}, u32[]{:S(2)}, u32[]{:S(2)}) collective-permute-start(f32[3,1,16,128]{3,2,1,0:T(8,128)} %copy.765), channel_id=1, source_target_pairs={{30,0},{0,2},{2,4},{4,6},{6,8},{8,10},{10,12},{12,14},{14,16},{16,... | collective-permute-start | bytes 73736 | tf_op jit(solution)/shard_map/ppermute | solution.py:57
  70.7 5.0 %copy-start.1 = (f32[19,2,16,128]{3,2,1,0:T(8,128)S(1)}, f32[19,2,16,128]{3,2,1,0:T(8,128)}, u32[]{:S(2)}) copy-start(f32[19,2,16,128]{3,2,1,0:T(8,128)} %gather_fusion) | copy-start | bytes 933892
  70.7 5.0 %copy-start.4 = (pred[2,16,128]{2,1,0:T(8,128)(4,1)S(1)}, pred[2,16,128]{2,1,0:T(8,128)(4,1)}, u32[]{:S(2)}) copy-start(pred[2,16,128]{2,1,0:T(8,128)(4,1)} %broadcast_compare_fusion) | copy-start | bytes 12292
  75.9 7.4 %collective-permute-start.2 = (f32[19,1,16,128]{3,2,1,0:T(8,128)S(1)}, f32[19,1,16,128]{3,2,1,0:T(8,128)S(1)}, u32[]{:S(2)}, u32[]{:S(2)}) collective-permute-start(f32[19,1,16,128]{3,2,1,0:T(8,128)S(1)} %get-tuple-element.109), channel_id=1, source_target_pairs={{0,2},{2,4},{4,6},{6,8},{8,10},{10,12},{12,14},{14,16},{16,18},{18... | collective-permute-start | bytes 466952 | tf_op jit(solution)/shard_map/ppermute | solution.py:48
  75.9 7.3 %collective-permute-start.3 = (f32[19,1,16,128]{3,2,1,0:T(8,128)S(1)}, f32[19,1,16,128]{3,2,1,0:T(8,128)S(1)}, u32[]{:S(2)}, u32[]{:S(2)}) collective-permute-start(f32[19,1,16,128]{3,2,1,0:T(8,128)S(1)} %get-tuple-element.110), channel_id=1, source_target_pairs={{2,0},{4,2},{6,4},{8,6},{10,8},{12,10},{14,12},{16,14},{18,16},{20... | collective-permute-start | bytes 466952 | tf_op jit(solution)/shard_map/ppermute | solution.py:49
  80.6 8.3 %copy-start.3 = (f32[3,2048]{1,0:T(4,128)}, f32[3,2048]{1,0:T(4,128)S(1)}, u32[]{:S(2)}) copy-start(f32[3,2048]{1,0:T(4,128)S(1)} %scatter-add.30) | copy-start | bytes 73732
  84.2 4.0 %collective-permute-start.4 = (f32[19,4,16,1]{0,2,3,1:T(8,128)S(1)}, f32[19,4,16,1]{0,2,3,1:T(8,128)S(1)}, u32[]{:S(2)}, u32[]{:S(2)}) collective-permute-start(f32[19,4,16,1]{0,2,3,1:T(8,128)S(1)} %copy.742), channel_id=1, source_target_pairs={{0,1},{1,0},{2,3},{3,2},{4,5},{5,4},{6,7},{7,6},{8,9},{9,8},{10,11... | collective-permute-start | bytes 14600 | tf_op jit(solution)/shard_map/ppermute | solution.py:48
  86.3 4.0 %collective-permute-start.5 = (f32[19,4,16,1]{0,2,3,1:T(8,128)S(1)}, f32[19,4,16,1]{0,2,3,1:T(8,128)S(1)}, u32[]{:S(2)}, u32[]{:S(2)}) collective-permute-start(f32[19,4,16,1]{0,2,3,1:T(8,128)S(1)} %copy.744), channel_id=1, source_target_pairs={{1,0},{0,1},{3,2},{2,3},{5,4},{4,5},{7,6},{6,7},{9,8},{8,9},{11,10... | collective-permute-start | bytes 14600 | tf_op jit(solution)/shard_map/ppermute | solution.py:49
  92.7 7.4 %collective-permute-start.6 = (f32[19,1,16,128]{3,2,1,0:T(8,128)S(1)}, f32[19,1,16,128]{3,2,1,0:T(8,128)S(1)}, u32[]{:S(2)}, u32[]{:S(2)}) collective-permute-start(f32[19,1,16,128]{3,2,1,0:T(8,128)S(1)} %get-tuple-element.102), channel_id=1, source_target_pairs={{0,2},{2,4},{4,6},{6,8},{8,10},{10,12},{12,14},{14,16},{16,18},{18... | collective-permute-start | bytes 466952 | tf_op jit(solution)/shard_map/ppermute | solution.py:48
  92.8 7.3 %collective-permute-start.7 = (f32[19,1,16,128]{3,2,1,0:T(8,128)S(1)}, f32[19,1,16,128]{3,2,1,0:T(8,128)S(1)}, u32[]{:S(2)}, u32[]{:S(2)}) collective-permute-start(f32[19,1,16,128]{3,2,1,0:T(8,128)S(1)} %get-tuple-element.101), channel_id=1, source_target_pairs={{2,0},{4,2},{6,4},{8,6},{10,8},{12,10},{14,12},{16,14},{18,16},{20... | collective-permute-start | bytes 466952 | tf_op jit(solution)/shard_map/ppermute | solution.py:49
  101.0 4.0 %collective-permute-start.8 = (f32[19,4,16,1]{0,2,3,1:T(8,128)S(1)}, f32[19,4,16,1]{0,2,3,1:T(8,128)S(1)}, u32[]{:S(2)}, u32[]{:S(2)}) collective-permute-start(f32[19,4,16,1]{0,2,3,1:T(8,128)S(1)} %copy.757), channel_id=1, source_target_pairs={{0,1},{1,0},{2,3},{3,2},{4,5},{5,4},{6,7},{7,6},{8,9},{9,8},{10,11... | collective-permute-start | bytes 14600 | tf_op jit(solution)/shard_map/ppermute | solution.py:48
  102.1 4.0 %collective-permute-start.9 = (f32[19,4,16,1]{0,2,3,1:T(8,128)S(1)}, f32[19,4,16,1]{0,2,3,1:T(8,128)S(1)}, u32[]{:S(2)}, u32[]{:S(2)}) collective-permute-start(f32[19,4,16,1]{0,2,3,1:T(8,128)S(1)} %copy.759), channel_id=1, source_target_pairs={{1,0},{0,1},{3,2},{2,3},{5,4},{4,5},{7,6},{6,7},{9,8},{8,9},{11,10... | collective-permute-start | bytes 14600 | tf_op jit(solution)/shard_map/ppermute | solution.py:49
  107.5 0.7 copy-start.6
where the time goes:
time: 109 us; the launch traced here: 108 us
  local copies, waits for them, and re-layouts  39.6 us (36%)
  other arithmetic  37.8 us (35%)
  starting transfers between devices  18.8 us (17%)
  waiting for transfers between devices  9.94 us (9%)
  between operations  2.18 us (2%)
    scatter-add x1, other arithmetic, body(): deposit = deposit.at[:, cell_index + plane].add(push * offset)  13 us
    scatter-add x1, other arithmetic, body(): deposit = deposit.at[:, cell_index].add(push * (1.0 - offset))  12.6 us
    ppermute x4, starting transfers between devices, extended_2(): after = lax.ppermute(leading, axis, down)  11 us
    gather x2, local copies, waits for them, and re-layouts, body(): ahead = jnp.take(extended, cell_index + plane, axis=1)  9.14 us
    gather x2, local copies, waits for them, and re-layouts, body(): here = jnp.take(extended, cell_index, axis=1)  9.14 us
    ppermute x4, waiting for transfers between devices, extended_2(): before = lax.ppermute(last, axis, up)  8.2 us
    unnamed x18, local copies, waits for them, and re-layouts  6.73 us
    ppermute x2, starting transfers between devices, shifted(): return lax.ppermute(block, axis, route)  5.5 us
  transfers between devices with their start and end apart: 10, of which 6 were waited for; matrix products, arithmetic and copies ran while one was open for 14% of the time, Pallas kernels for 0%

commit v1 on v0

v1 whole, which is shorter than its diff:
```python
import functools

import jax
import jax.numpy as jnp
import numpy as np
from jax import lax
from jax.experimental import pallas as pl
from jax.experimental.pallas import tpu as pltpu
from jax.sharding import PartitionSpec as P

SUBSTEPS = 2

LATTICE = [
    (0, 0, 0),
    (1, 0, 0),
    (-1, 0, 0),
    (0, 1, 0),
    (0, -1, 0),
    (0, 0, 1),
    (0, 0, -1),
    (1, 1, 0),
    (-1, -1, 0),
    (1, -1, 0),
    (-1, 1, 0),
    (1, 0, 1),
    (-1, 0, -1),
    (1, 0, -1),
    (-1, 0, 1),
    (0, 1, 1),
    (0, -1, -1),
    (0, 1, -1),
    (0, -1, 1),
]
WEIGHTS = [1.0 / 3.0] + [1.0 / 18.0] * 6 + [1.0 / 36.0] * 12
relax_time = 0.6
coupling = 0.5
settle = 0.02
body_force = 0.0001

PAIRS = [(k, k + 1) for k in range(1, 19, 2)]
XP = [k for k in range(19) if LATTICE[k][0] == 1]
XM = [k for k in range(19) if LATTICE[k][0] == -1]
X0 = [k for k in range(19) if LATTICE[k][0] == 0]
ORDER = XP + XM + X0
PLACE = {k: i for i, k in enumerate(ORDER)}
ZP = [k for k in range(19) if LATTICE[k][2] == 1]
ZM = [k for k in range(19) if LATTICE[k][2] == -1]
LANES = {}
for _k in ZP + ZM:
    for _x in range(2):
        LANES[_k, _x] = len(LANES)


def halves(value):
    high = value.astype(jnp.bfloat16).astype(jnp.float32)
    return high, value - high


def total_of(terms):
    while len(terms) > 1:
        terms = [
            terms[i] + terms[i + 1] if i + 1 < len(terms) else terms[i]
            for i in range(0, len(terms), 2)
        ]
    return terms[0]


def moments(f):
    rho = total_of(list(f))
    mom = []
    for d in range(3):
        up = [f[k] for k in range(19) if LATTICE[k][d] == 1]
        down = [f[k] for k in range(19) if LATTICE[k][d] == -1]
        mom.append(total_of(up) - total_of(down))
    return rho, mom


def kernel(
    n_gx, n_gz,
    pops_in, solid_in, idx_in, off_in, vel_in, mass_in, counts_in,
    pops_out, vel_out,
    f_v, solid_v, idx_v, off_v, vel_v, mass_v, counts_v, nv_v, out_v, post_v,
    onehot_v, coef_v, vsend, vrecv, ssend, srecv, xp_recv, xm_recv, zsend, zrecv,
    in_sem, out_sem, vs_sem, vr_sem, ss_sem, sr_sem, x_ss, x_rs, z_ss, z_rs,
):
    gx, gz = lax.axis_index("gx"), lax.axis_index("gz")
    right, left = lax.rem(gx + 1, n_gx), lax.rem(gx + n_gx - 1, n_gx)
    xpos = {-1: left, 0: gx, 1: right}
    zdirs = (1,) if n_gz == 2 else (1, -1)
    zpos = {1: lax.rem(gz + 1, n_gz), -1: lax.rem(gz + n_gz - 1, n_gz), 0: gz}

    loads = [
        pltpu.make_async_copy(src, dst, in_sem.at[i])
        for i, (src, dst) in enumerate(
            [
                (pops_in, f_v),
                (idx_in, idx_v),
                (off_in, off_v),
                (mass_in, mass_v),
                (vel_in, vel_v),
                (counts_in, counts_v),
                (solid_in, solid_v),
            ]
        )
    ]
    for load in loads:
        load.start()

    peers = [(dx, dz) for dz in (0,) + zdirs for dx in (-1, 0, 1) if (dx, dz) != (0, 0)]
    barrier = pltpu.get_barrier_semaphore()
    for dx, dz in peers:
        pl.semaphore_signal(
            barrier,
            inc=1,
            device_id={"gx": xpos[dx], "gz": zpos[dz]},
            device_id_type=pl.DeviceIdType.MESH,
        )

    def send(src, dst, send_sem, recv_sem, dx, dz):
        copy = pltpu.make_async_remote_copy(
            src_ref=src,
            dst_ref=dst,
            send_sem=send_sem,
            recv_sem=recv_sem,
            device_id={"gx": xpos[dx], "gz": zpos[dz]},
            device_id_type=pl.DeviceIdType.MESH,
        )
        copy.start()
        return copy

    sent = []
    ny, nz = f_v.shape[2], f_v.shape[3]
    slots = idx_v.shape[0] * idx_v.shape[1]
    zbits, ybits = nz.bit_length() - 1, ny.bit_length() - 1

    for load in loads[1:6]:
        load.wait()

    def row(ref):
        return jnp.concatenate([ref[j : j + 1, :] for j in range(ref.shape[0])], axis=1)

    idx, off, mass = row(idx_v), row(off_v), row(mass_v)
    live = lax.broadcasted_iota(jnp.int32, (1, slots), 1) < counts_v[...]
    live = jnp.where(live, 1.0, 0.0).astype(jnp.float32)
    yidx = (idx >> zbits) & (ny - 1)
    key = ((idx >> (zbits + ybits)) << zbits) | (idx & (nz - 1))
    onehot_v[...] = jnp.where(
        lax.broadcasted_iota(jnp.int32, (2 * nz, slots), 0) == key, 1.0, 0.0
    ).astype(jnp.bfloat16)
    ymask = lax.broadcasted_iota(jnp.int32, (ny, slots), 0) == yidx
    near = 1.0 - off
    weight = (coupling * live) * mass
    wnear, wfar = weight * near, weight * off
    vel = [vel_v[d : d + 1, :] for d in range(3)]
    channels = [wnear * near, wnear * off, wfar * off]
    channels += [wnear * vel[d] for d in range(3)]
    channels += [wfar * vel[d] for d in range(3)]
    n_ch = len(channels)
    for c, channel in enumerate(channels):
        for h, part in enumerate(halves(channel)):
            at = (h * n_ch + c) * ny
            coef_v[at : at + ny, :] = jnp.where(ymask, part, 0.0).astype(jnp.bfloat16)

    loads[0].wait()
    f = [f_v[k] for k in range(19)]
    rho, mom = moments(f)
    inv = 1.0 / rho
    v = [m * inv for m in mom]
    for d in range(3):
        vsend[d] = v[d][0]
    pl.semaphore_wait(barrier, len(peers))
    v_copy = send(vsend, vrecv, vs_sem, vr_sem, -1, 0)
    sent.append(v_copy)

    sums = lax.dot_general(
        coef_v[...],
        onehot_v[...],
        (((1,), (1,)), ((), ())),
        preferred_element_type=jnp.float32,
    )
    sums = sums[: n_ch * ny] + sums[n_ch * ny :]

    def moment(c, x):
        return sums[c * ny : (c + 1) * ny, x * nz : (x + 1) * nz]

    a = [moment(0, x) for x in range(2)]
    b = [moment(1, x) for x in range(2)]
    e = [moment(2, x) for x in range(2)]
    q = [[moment(3 + d, x) for x in range(2)] for d in range(3)]
    r = [[moment(6 + d, x) for x in range(2)] for d in range(3)]
    for d in range(3):
        ssend[d] = r[d][1] - b[1] * v[d][1]
    ssend[3] = e[1]
    s_copy = send(ssend, srecv, ss_sem, sr_sem, 1, 0)
    sent.append(s_copy)

    loads[6].wait()
    solid = solid_v[...] > 0
    lane = lax.broadcasted_iota(jnp.int32, (ny, nz), 1)

    v_copy.wait_recv()
    s_copy.wait_recv()
    force = []
    for d in range(3):
        extra = body_force if d == 0 else 0.0
        first = q[d][0] - a[0] * v[d][0] - b[0] * v[d][1]
        first = first + (srecv[d] - srecv[3] * v[d][0]) + extra
        second = q[d][1] - a[1] * v[d][1] - b[1] * vrecv[d]
        second = second + (r[d][0] - b[0] * v[d][0] - e[0] * v[d][1]) + extra
        force.append(jnp.stack([first, second]) * relax_time)

    def particles():
        flows = []
        here = [jnp.concatenate([v[d][0], v[d][1]], axis=1) for d in range(3)]
        ahead = [jnp.concatenate([v[d][1], vrecv[d]], axis=1) for d in range(3)]
        table = jnp.concatenate(here + ahead, axis=0)
        high, low = halves(table)
        oh = onehot_v[...]
        found = jnp.dot(high.astype(jnp.bfloat16), oh, preferred_element_type=jnp.float32)
        found = found + jnp.dot(low.astype(jnp.bfloat16), oh, preferred_element_type=jnp.float32)
        for d in range(3):
            mix = near * found[d * ny : (d + 1) * ny] + off * found[(3 + d) * ny : (4 + d) * ny]
            flow = jnp.sum(jnp.where(ymask, mix, 0.0), axis=0, keepdims=True)
            new = vel[d] + coupling * live * (flow - vel[d])
            if d == 1:
                new = new - settle * live
            nv_v[d : d + 1, :] = new
        copy = pltpu.make_async_copy(nv_v, vel_out, out_sem.at[1])
        copy.start()
        return copy

    for step in range(SUBSTEPS):
        if step:
            rho, mom = moments(f)
            inv = 1.0 / rho
        post = post_v.at[step]
        u = [(mom[d] + force[d]) * inv for d in range(3)]
        usq = u[0] * u[0] + u[1] * u[1] + u[2] * u[2]
        scale = rho * (1.0 / relax_time)
        base = scale * (1.0 - 1.5 * usq)
        keep = 1.0 - 1.0 / relax_time
        by = {}

        def pair(k, o):
            w = WEIGHTS[k]
            along = total_of(
                [u[d] if LATTICE[k][d] == 1 else -u[d] for d in range(3) if LATTICE[k][d]]
            )
            lift = scale * along
            even = w * base + (4.5 * w) * (lift * along)
            odd = (3.0 * w) * lift
            by[k] = jnp.where(solid, f[o], keep * f[k] + (even + odd))
            by[o] = jnp.where(solid, f[k], keep * f[o] + (even - odd))
            post[PLACE[k]] = by[k]
            post[PLACE[o]] = by[o]

        for k, o in PAIRS:
            if LATTICE[k][0]:
                pair(k, o)
        xp_copy = send(
            post.at[0:5, 1], xp_recv.at[step], x_ss.at[step, 0], x_rs.at[step, 0], 1, 0
        )
        xm_copy = send(
            post.at[5:10, 0], xm_recv.at[step], x_ss.at[step, 1], x_rs.at[step, 1], -1, 0
        )
        for k, o in PAIRS:
            if not LATTICE[k][0] and LATTICE[k][2]:
                pair(k, o)
        packed = jnp.zeros((ny, nz), jnp.float32)
        for (k, x), at in LANES.items():
            edge = nz - 1 if LATTICE[k][2] == 1 else 0
            column = jnp.broadcast_to(by[k][x][:, edge : edge + 1], (ny, nz))
            packed = jnp.where(lane == at, column, packed)
        zsend[step] = packed
        z_copies = []
        for s, dz in enumerate(zdirs):
            for dx in (-1, 1, 0):
                z_copies.append(
                    send(
                        zsend.at[step],
                        zrecv.at[step, s, 1 - dx],
                        z_ss.at[step, s, 1 - dx],
                        z_rs.at[step, s, 1 - dx],
                        dx,
                        dz,
                    )
                )
        for k, o in PAIRS:
            if not LATTICE[k][0] and not LATTICE[k][2]:
                pair(k, o)
        by[0] = jnp.where(solid, f[0], keep * f[0] + WEIGHTS[0] * base)
        if step == 0:
            vel_copy = particles()
        xp_copy.wait_recv()
        xm_copy.wait_recv()
        for copy in z_copies:
            copy.wait_recv()
        sent += [xp_copy, xm_copy] + z_copies
        nf = []
        for k in range(19):
            cx, cy, cz = LATTICE[k]
            if cx == 1:
                planes = [(xp_recv[step, XP.index(k)], 0, 1), (by[k][0], 1, 0)]
            elif cx == -1:
                planes = [(by[k][1], 1, 1), (xm_recv[step, XM.index(k)], 2, 0)]
            else:
                planes = [(by[k][0], 1, 0), (by[k][1], 1, 1)]
            done = []
            for plane, source, x in planes:
                if cz:
                    s = 0 if cz == 1 else len(zdirs) - 1
                    at = LANES[k, x]
                    column = zrecv[step, s, source, :, at : at + 1]
                    plane = pltpu.roll(plane, 1 if cz == 1 else nz - 1, 1)
                    plane = jnp.where(
                        lane == (0 if cz == 1 else nz - 1),
                        jnp.broadcast_to(column, (ny, nz)),
                        plane,
                    )
                if cy:
                    plane = pltpu.roll(plane, 1 if cy == 1 else ny - 1, 0)
                done.append(plane)
            if step == SUBSTEPS - 1:
                out_v[k, 0] = done[0]
                out_v[k, 1] = done[1]
            else:
                nf.append(jnp.stack(done))
        f = nf

    out_copy = pltpu.make_async_copy(out_v, pops_out, out_sem.at[0])
    out_copy.start()
    for copy in sent:
        copy.wait_send()
    vel_copy.wait()
    out_copy.wait()


def body(n_gx, n_gz, populations, solid, cell_index, offset, velocity, mass, counts):
    depth_x, ny, nz = populations.shape[1:]
    slots = cell_index.shape[0]
    rows = (slots // nz, nz)
    nzs = 1 if n_gz == 2 else 2
    f32, vmem, dma = jnp.float32, pltpu.VMEM, pltpu.SemaphoreType.DMA
    return pl.pallas_call(
        functools.partial(kernel, n_gx, n_gz),
        out_shape=(
            jax.ShapeDtypeStruct(populations.shape, f32),
            jax.ShapeDtypeStruct(velocity.shape, f32),
        ),
        in_specs=[pl.BlockSpec(memory_space=pl.ANY)] * 7,
        out_specs=[pl.BlockSpec(memory_space=pl.ANY)] * 2,
        scratch_shapes=[
            vmem(populations.shape, f32),
            vmem(solid.shape, jnp.int32),
            vmem(rows, jnp.int32),
            vmem(rows, f32),
            vmem(velocity.shape, f32),
            vmem(rows, f32),
            vmem((1, 1), jnp.int32),
            vmem(velocity.shape, f32),
            vmem(populations.shape, f32),
            vmem((SUBSTEPS,) + populations.shape, f32),
            vmem((2 * nz, slots), jnp.bfloat16),
            vmem((18 * ny, slots), jnp.bfloat16),
            vmem((3, ny, nz), f32),
            vmem((3, ny, nz), f32),
            vmem((4, ny, nz), f32),
            vmem((4, ny, nz), f32),
            vmem((SUBSTEPS, 5, ny, nz), f32),
            vmem((SUBSTEPS, 5, ny, nz), f32),
            vmem((SUBSTEPS, ny, nz), f32),
            vmem((SUBSTEPS, nzs, 3, ny, nz), f32),
            dma((7,)),
            dma((2,)),
            dma,
            dma,
            dma,
            dma,
            dma((SUBSTEPS, 2)),
            dma((SUBSTEPS, 2)),
            dma((SUBSTEPS, nzs, 3)),
            dma((SUBSTEPS, nzs, 3)),
        ],
        compiler_params=pltpu.CompilerParams(
            collective_id=0, has_side_effects=True, vmem_limit_bytes=32 * 1024 * 1024
        ),
    )(
        populations,
        solid,
        cell_index.reshape(rows),
        offset.reshape(rows),
        velocity,
        mass.reshape(rows),
        counts,
    )


def solution(mesh):
    return jax.shard_map(
        functools.partial(body, mesh.shape["gx"], mesh.shape["gz"]),
        mesh=mesh,
        in_specs=(
            P(None, "gx", None, "gz"),
            P("gx", None, "gz"),
            P(("gx", "gz")),
            P(("gx", "gz")),
            P(None, ("gx", "gz")),
            P(("gx", "gz")),
            P("gx", "gz"),
        ),
        out_specs=(P(None, "gx", None, "gz"), P(None, ("gx", "gz"))),
        check_vma=False,
    )
```

time: 109 us -> 27.3 us (0.25)
  other arithmetic: 37.8 us -> 0 us
  local copies, waits for them, and re-layouts: 39.6 us -> 5.86 us
  Pallas kernels: 0 us -> 19.7 us
  starting transfers between devices: 18.8 us -> 0 us
  waiting for transfers between devices: 9.94 us -> 0 us
    scatter-add x3 -> x0, other arithmetic: 26.3 us -> none  [the longest x1 13 us: body(): deposit = deposit.at[:, cell_index + plane].add(push * offset)]
    gather x6 -> x0, local copies, waits for them, and re-layouts: 20.4 us -> none  [the longest x2 9.14 us: body(): ahead = jnp.take(extended, cell_index + plane, axis=1)]
    pallas_call x0 -> x1, Pallas kernels: none -> 19.7 us  [body(): pl.pallas_call(functools.partial(kernel, n_gx, n_gz), out_shape=(jax.Shap...]
    ppermute x10 -> x0, starting transfers between devices: 18.8 us -> none  [the longest x4 11 us: extended_2(): after = lax.ppermute(leading, axis, down)]
    ppermute x10 -> x0, waiting for transfers between devices: 9.94 us -> none  [the longest x4 8.2 us: extended_2(): before = lax.ppermute(last, axis, up)]
    slice x45 -> x0, local copies, waits for them, and re-layouts: 5.72 us -> none  [the longest x5 1.54 us: extended_2(): leading = lax.slice_in_dim(value, 0, width, axis=dim)]
    ppermute x4 -> x0, local copies, waits for them, and re-layouts: 2.83 us -> none  [the longest x2 1.42 us: extended_2(): before = lax.ppermute(last, axis, up)]
    mul x2 -> x0, local copies, waits for them, and re-layouts: 2.73 us -> none  [the longest x1 1.38 us: body(): deposit = deposit.at[:, cell_index].add(push * (1.0 - offset))]
  transfers between devices with their start and end apart: 10 -> 0, of which waited for: 6 -> 0; matrix products, arithmetic and copies ran while one was open for 14% -> 0% of each run, Pallas kernels for 0% -> 0%
where the time goes in v1:
time: 27.3 us; the launch traced here: 26.9 us
  Pallas kernels  19.7 us (72%)
  local copies, waits for them, and re-layouts  5.86 us (21%)
  between operations  1.3 us (5%)
    pallas_call x1, Pallas kernels, body(): pl.pallas_call(functools.partial(kernel, n_gx, n_gz), out_shape=(jax.Shap...  19.7 us
    unnamed x14, local copies, waits for them, and re-layouts  5.86 us

profile of v1, /device:TPU:0, one launch (start us, length us, event | category | flops | bytes accessed | tf_op | source)
XLA Modules:
  0.0 26.9 jit_solution(7961361881340093771)
XLA Ops:
  1.3 0.0 copy-start
  1.3 1.0 %copy-done = f32[19,2,16,128]{3,2,1,0:T(8,128)S(1)} copy-done((f32[19,2,16,128]{3,2,1,0:T(8,128)S(1)}, f32[19,2,16,128]{3,2,1,0:T(8,128)}, u32[]{:S(2)}) %copy-start) | copy-done | bytes 311320
  2.2 0.0 copy-start.1
  2.2 0.8 %copy-done.1 = f32[3,2048]{1,0:T(4,128)S(1)} copy-done((f32[3,2048]{1,0:T(4,128)S(1)}, f32[3,2048]{1,0:T(4,128)}, u32[]{:S(2)}) %copy-start.1) | copy-done | bytes 24600
  3.0 0.0 copy-start.2
  3.0 0.7 %copy-done.2 = s32[2,16,128]{2,1,0:T(8,128)S(1)} copy-done((s32[2,16,128]{2,1,0:T(8,128)S(1)}, s32[2,16,128]{2,1,0:T(8,128)}, u32[]{:S(2)}) %copy-start.2) | copy-done | bytes 16408
  3.7 0.0 copy-start.3
  3.7 0.7 %copy-done.3 = s32[2048]{0:T(1024)S(1)} copy-done((s32[2048]{0:T(1024)S(1)}, s32[2048]{0:T(1024)}, u32[]{:S(2)}) %copy-start.3) | copy-done | bytes 8216
  4.4 0.0 copy-start.4
  4.4 0.7 %copy-done.4 = f32[2048]{0:T(1024)S(1)} copy-done((f32[2048]{0:T(1024)S(1)}, f32[2048]{0:T(1024)}, u32[]{:S(2)}) %copy-start.4) | copy-done | bytes 8216
  5.1 0.0 copy-start.5
  5.1 0.7 %copy-done.5 = f32[2048]{0:T(1024)S(1)} copy-done((f32[2048]{0:T(1024)S(1)}, f32[2048]{0:T(1024)}, u32[]{:S(2)}) %copy-start.5) | copy-done | bytes 8216
  5.8 19.7 %shard_map.86 = (f32[19,2,16,128]{3,2,1,0:T(8,128)S(1)}, f32[3,2048]{1,0:T(4,128)S(1)}) custom-call(f32[19,2,16,128]{3,2,1,0:T(8,128)S(1)} %copy-done, s32[2,16,128]{2,1,0:T(8,128)S(1)} %copy-done.2, s32[16,128]{1,0:T(8,128)S(1)} %bitcast.3, f32[16,128]{1,0:T(8,128)S(1)} %bitcast.4, f32[3,2048]{1,0:T(4,128)S(1)} %copy-done.1, f32[16,128]{1,0:T(8,128)S(1)} %bitcast.5, ...), custom_call_target="tpu_custom_call" | custom-call | tf_op jit(solution)/shard_map/pallas_call | solution.py:344
  25.6 0.7 %copy.12 = f32[19,2,16,128]{3,2,1,0:T(8,128)} copy(f32[19,2,16,128]{3,2,1,0:T(8,128)S(1)} %get-tuple-element.4) | data formatting | bytes 622592
  26.3 0.6 %copy.13 = f32[3,2048]{1,0:T(4,128)} copy(f32[3,2048]{1,0:T(4,128)S(1)} %get-tuple-element.5) | data formatting | bytes 49152
Async XLA Ops:
  1.3 1.0 %copy-start = (f32[19,2,16,128]{3,2,1,0:T(8,128)S(1)}, f32[19,2,16,128]{3,2,1,0:T(8,128)}, u32[]{:S(2)}) copy-start(f32[19,2,16,128]{3,2,1,0:T(8,128)} %pops_in.1) | copy-start | bytes 933892
  2.2 0.8 %copy-start.1 = (f32[3,2048]{1,0:T(4,128)S(1)}, f32[3,2048]{1,0:T(4,128)}, u32[]{:S(2)}) copy-start(f32[3,2048]{1,0:T(4,128)} %vel_in.1) | copy-start | bytes 73732
  3.0 0.7 %copy-start.2 = (s32[2,16,128]{2,1,0:T(8,128)S(1)}, s32[2,16,128]{2,1,0:T(8,128)}, u32[]{:S(2)}) copy-start(s32[2,16,128]{2,1,0:T(8,128)} %solid_in.1) | copy-start | bytes 49156
  3.7 0.7 %copy-start.3 = (s32[2048]{0:T(1024)S(1)}, s32[2048]{0:T(1024)}, u32[]{:S(2)}) copy-start(s32[2048]{0:T(1024)} %param.9) | copy-start | bytes 24580
  4.4 0.7 %copy-start.4 = (f32[2048]{0:T(1024)S(1)}, f32[2048]{0:T(1024)}, u32[]{:S(2)}) copy-start(f32[2048]{0:T(1024)} %param.10) | copy-start | bytes 24580
  5.1 0.7 %copy-start.5 = (f32[2048]{0:T(1024)S(1)}, f32[2048]{0:T(1024)}, u32[]{:S(2)}) copy-start(f32[2048]{0:T(1024)} %param.12) | copy-start | bytes 24580

commit v2 on v1

--- a/solution.py
+++ b/solution.py
@@ -78,10 +78,10 @@
 def kernel(
     n_gx, n_gz,
     pops_in, solid_in, idx_in, off_in, vel_in, mass_in, counts_in,
-    pops_out, vel_out,
-    f_v, solid_v, idx_v, off_v, vel_v, mass_v, counts_v, nv_v, out_v, post_v,
+    out_v, nv_v,
+    f_v, solid_v, idx_v, off_v, vel_v, mass_v, counts_v, post_v,
     onehot_v, coef_v, vsend, vrecv, ssend, srecv, xp_recv, xm_recv, zsend, zrecv,
-    in_sem, out_sem, vs_sem, vr_sem, ss_sem, sr_sem, x_ss, x_rs, z_ss, z_rs,
+    in_sem, vs_sem, vr_sem, ss_sem, sr_sem, x_ss, x_rs, z_ss, z_rs,
 ):
     gx, gz = lax.axis_index("gx"), lax.axis_index("gz")
     right, left = lax.rem(gx + 1, n_gx), lax.rem(gx + n_gx - 1, n_gx)
@@ -225,9 +225,6 @@
             if d == 1:
                 new = new - settle * live
             nv_v[d : d + 1, :] = new
-        copy = pltpu.make_async_copy(nv_v, vel_out, out_sem.at[1])
-        copy.start()
-        return copy
 
     for step in range(SUBSTEPS):
         if step:
@@ -290,7 +287,7 @@
                 pair(k, o)
         by[0] = jnp.where(solid, f[0], keep * f[0] + WEIGHTS[0] * base)
         if step == 0:
-            vel_copy = particles()
+            particles()
         xp_copy.wait_recv()
         xm_copy.wait_recv()
         for copy in z_copies:
@@ -327,12 +324,19 @@
                 nf.append(jnp.stack(done))
         f = nf
 
-    out_copy = pltpu.make_async_copy(out_v, pops_out, out_sem.at[0])
-    out_copy.start()
     for copy in sent:
         copy.wait_send()
-    vel_copy.wait()
-    out_copy.wait()
+
+
+def store(a_in, b_in, a_out, b_out, sems):
+    copies = [
+        pltpu.make_async_copy(a_in, a_out, sems.at[0]),
+        pltpu.make_async_copy(b_in, b_out, sems.at[1]),
+    ]
+    for copy in copies:
+        copy.start()
+    for copy in copies:
+        copy.wait()
 
 
 def body(n_gx, n_gz, populations, solid, cell_index, offset, velocity, mass, counts):
@@ -341,14 +345,16 @@
     rows = (slots // nz, nz)
     nzs = 1 if n_gz == 2 else 2
     f32, vmem, dma = jnp.float32, pltpu.VMEM, pltpu.SemaphoreType.DMA
-    return pl.pallas_call(
+    shapes = (
+        jax.ShapeDtypeStruct(populations.shape, f32),
+        jax.ShapeDtypeStruct(velocity.shape, f32),
+    )
+    held = pl.pallas_call(
         functools.partial(kernel, n_gx, n_gz),
-        out_shape=(
-            jax.ShapeDtypeStruct(populations.shape, f32),
-            jax.ShapeDtypeStruct(velocity.shape, f32),
-        ),
-        in_specs=[pl.BlockSpec(memory_space=pl.ANY)] * 7,
-        out_specs=[pl.BlockSpec(memory_space=pl.ANY)] * 2,
+        out_shape=shapes,
+        in_specs=[pl.BlockSpec(memory_space=pltpu.HBM)] * 6
+        + [pl.BlockSpec(memory_space=pl.ANY)],
+        out_specs=[pl.BlockSpec(memory_space=pltpu.VMEM)] * 2,
         scratch_shapes=[
             vmem(populations.shape, f32),
             vmem(solid.shape, jnp.int32),
@@ -357,8 +363,6 @@
             vmem(velocity.shape, f32),
             vmem(rows, f32),
             vmem((1, 1), jnp.int32),
-            vmem(velocity.shape, f32),
-            vmem(populations.shape, f32),
             vmem((SUBSTEPS,) + populations.shape, f32),
             vmem((2 * nz, slots), jnp.bfloat16),
             vmem((18 * ny, slots), jnp.bfloat16),
@@ -371,7 +375,6 @@
             vmem((SUBSTEPS, ny, nz), f32),
             vmem((SUBSTEPS, nzs, 3, ny, nz), f32),
             dma((7,)),
-            dma((2,)),
             dma,
             dma,
             dma,
@@ -385,14 +388,27 @@
             collective_id=0, has_side_effects=True, vmem_limit_bytes=32 * 1024 * 1024
         ),
     )(
-        populations,
-        solid,
-        cell_index.reshape(rows),
-        offset.reshape(rows),
-        velocity,
-        mass.reshape(rows),
+        *[
+            pltpu.with_memory_space_constraint(value, pltpu.HBM)
+            for value in (
+                populations,
+                solid,
+                cell_index.reshape(rows),
+                offset.reshape(rows),
+                velocity,
+                mass.reshape(rows),
+            )
+        ],
         counts,
     )
+    return pl.pallas_call(
+        store,
+        out_shape=shapes,
+        in_specs=[pl.BlockSpec(memory_space=pltpu.VMEM)] * 2,
+        out_specs=[pl.BlockSpec(memory_space=pltpu.HBM)] * 2,
+        scratch_shapes=[dma((2,))],
+        compiler_params=pltpu.CompilerParams(vmem_limit_bytes=2 * 1024 * 1024),
+    )(*held)
 
 
 def solution(mesh):

time: 27.3 us -> 21.7 us (0.79)
  local copies, waits for them, and re-layouts: 5.86 us -> 0 us
  Pallas kernels: 19.7 us -> 20.3 us
    unnamed x14 -> x0, local copies, waits for them, and re-layouts: 5.86 us -> none
    pallas_call x1 -> x2, Pallas kernels: 19.7 us -> 20.3 us  [the longest x1 19.5 us: body(): pl.pallas_call(functools.partial(kernel, n_gx, n_gz), out_shape=shapes, i...]
where the time goes in v2:
time: 21.7 us; the launch traced here: 21.5 us
  Pallas kernels  20.3 us (94%)
  between operations  1.29 us (6%)
    pallas_call x1, Pallas kernels, body(): pl.pallas_call(functools.partial(kernel, n_gx, n_gz), out_shape=shapes, i...  19.5 us
    pallas_call x1, Pallas kernels, body(): pl.pallas_call(store, out_shape=shapes, in_specs=[pl.BlockSpec(memory_spa...  0.74 us

profile of v2, /device:TPU:0, one launch (start us, length us, event | category | flops | bytes accessed | tf_op | source)
XLA Modules:
  0.0 21.5 jit_solution(15077732683747492659)
XLA Ops:
  1.3 19.5 %shard_map.86 = (f32[19,2,16,128]{3,2,1,0:T(8,128)S(1)}, f32[3,2048]{1,0:T(4,128)S(1)}) custom-call(f32[19,2,16,128]{3,2,1,0:T(8,128)} %pops_in.1, s32[2,16,128]{2,1,0:T(8,128)} %solid_in.1, s32[16,128]{1,0:T(8,128)} %bitcast.3, f32[16,128]{1,0:T(8,128)} %bitcast.4, f32[3,2048]{1,0:T(4,128)} %vel_in.1, f32[16,128]{1,0:T(8,128)} %bitcast.5, ...), custom_call_target="tpu_custom_call" | custom-call | tf_op jit(solution)/shard_map/pallas_call | solution.py:352
  20.8 0.7 %shard_map.87 = (f32[19,2,16,128]{3,2,1,0:T(8,128)}, f32[3,2048]{1,0:T(4,128)}) custom-call(f32[19,2,16,128]{3,2,1,0:T(8,128)S(1)} %get-tuple-element.4.a_in, f32[3,2048]{1,0:T(4,128)S(1)} %get-tuple-element.5.b_in), custom_call_target="tpu_custom_call" | custom-call | tf_op jit(solution)/shard_map/pallas_call | solution.py:404

commit v3 on v2

v3 whole, which is shorter than its diff:
```python
import functools

import jax
import jax.numpy as jnp
from jax import lax
from jax.experimental import pallas as pl
from jax.experimental.pallas import tpu as pltpu
from jax.sharding import PartitionSpec as P

LATTICE = [
    (0, 0, 0),
    (1, 0, 0),
    (-1, 0, 0),
    (0, 1, 0),
    (0, -1, 0),
    (0, 0, 1),
    (0, 0, -1),
    (1, 1, 0),
    (-1, -1, 0),
    (1, -1, 0),
    (-1, 1, 0),
    (1, 0, 1),
    (-1, 0, -1),
    (1, 0, -1),
    (-1, 0, 1),
    (0, 1, 1),
    (0, -1, -1),
    (0, 1, -1),
    (0, -1, 1),
]
WEIGHTS = [1.0 / 3.0] + [1.0 / 18.0] * 6 + [1.0 / 36.0] * 12
relax_time = 0.6
coupling = 0.5
settle = 0.02
body_force = 0.0001

OPPOSITE = [0] + [k + 1 if k % 2 else k - 1 for k in range(1, 19)]
XP = [k for k in range(19) if LATTICE[k][0] == 1]
XM = [k for k in range(19) if LATTICE[k][0] == -1]
ZP = [k for k in range(19) if LATTICE[k][2] == 1]
ZM = [k for k in range(19) if LATTICE[k][2] == -1]
LANES = {}
for _k in ZP + ZM:
    for _x in range(2):
        LANES[_k, _x] = len(LANES)


def halves(value):
    high = value.astype(jnp.bfloat16).astype(jnp.float32)
    return high, value - high


def total_of(terms):
    while len(terms) > 1:
        terms = [
            terms[i] + terms[i + 1] if i + 1 < len(terms) else terms[i]
            for i in range(0, len(terms), 2)
        ]
    return terms[0]


def moments(f):
    rho = total_of(list(f))
    mom = []
    for d in range(3):
        up = [f[k] for k in range(19) if LATTICE[k][d] == 1]
        down = [f[k] for k in range(19) if LATTICE[k][d] == -1]
        mom.append(total_of(up) - total_of(down))
    return rho, mom


def pair_terms(k, u, scale, base):
    w = WEIGHTS[k]
    along = total_of(
        [u[d] if LATTICE[k][d] == 1 else -u[d] for d in range(3) if LATTICE[k][d]]
    )
    lift = scale * along
    return w * base + (4.5 * w) * (lift * along), (3.0 * w) * lift


def collide(ks, kept, m, inv, scale):
    u = [value * inv for value in m]
    base = scale * (1.0 - 1.5 * (u[0] * u[0] + u[1] * u[1] + u[2] * u[2]))
    out, terms = {}, {}
    for k in ks:
        if k == 0:
            out[0] = kept[0] + WEIGHTS[0] * base
            continue
        first = k if k % 2 else k - 1
        if first not in terms:
            terms[first] = pair_terms(first, u, scale, base)
        even, odd = terms[first]
        out[k] = kept[k] + (even + odd if k == first else even - odd)
    return out


def kernel(
    n_gx, n_gz,
    pops_in, solid_in, idx_in, off_in, vel_in, mass_in, counts_in,
    out_v, nv_v,
    f_v, solid_v, idx_v, off_v, vel_v, mass_v, counts_v,
    onehot_v, coef_v, a1s, a1r, a2s, a2r, b1s, b1r, b2s, b2r,
    xp_send, xm_send, xp_recv, xm_recv, zsend, zrecv,
    in_sem, r_ss, r_rs, x_ss, x_rs, z_ss, z_rs,
):
    gx, gz = lax.axis_index("gx"), lax.axis_index("gz")
    right, left = lax.rem(gx + 1, n_gx), lax.rem(gx + n_gx - 1, n_gx)
    xpos = {-1: left, 0: gx, 1: right}
    zdirs = (1,) if n_gz == 2 else (1, -1)
    zpos = {1: lax.rem(gz + 1, n_gz), -1: lax.rem(gz + n_gz - 1, n_gz), 0: gz}

    loads = [
        pltpu.make_async_copy(src, dst, in_sem.at[i])
        for i, (src, dst) in enumerate(
            [
                (pops_in, f_v),
                (solid_in, solid_v),
                (idx_in, idx_v),
                (off_in, off_v),
                (mass_in, mass_v),
                (vel_in, vel_v),
                (counts_in, counts_v),
            ]
        )
    ]
    for load in loads:
        load.start()

    peers = [(dx, dz) for dz in (0,) + zdirs for dx in (-1, 0, 1) if (dx, dz) != (0, 0)]
    barrier = pltpu.get_barrier_semaphore()
    for dx, dz in peers:
        pl.semaphore_signal(
            barrier,
            inc=1,
            device_id={"gx": xpos[dx], "gz": zpos[dz]},
            device_id_type=pl.DeviceIdType.MESH,
        )

    sent = []

    def send(src, dst, send_sem, recv_sem, dx, dz):
        copy = pltpu.make_async_remote_copy(
            src_ref=src,
            dst_ref=dst,
            send_sem=send_sem,
            recv_sem=recv_sem,
            device_id={"gx": xpos[dx], "gz": zpos[dz]},
            device_id_type=pl.DeviceIdType.MESH,
        )
        copy.start()
        sent.append(copy)
        return copy

    def send_rim(step):
        return [
            send(
                zsend.at[step],
                zrecv.at[step, s, 1 - dx],
                z_ss.at[step, s, 1 - dx],
                z_rs.at[step, s, 1 - dx],
                dx,
                dz,
            )
            for s, dz in enumerate(zdirs)
            for dx in (-1, 1, 0)
        ]

    ny, nz = f_v.shape[2], f_v.shape[3]
    slots = idx_v.shape[0] * idx_v.shape[1]
    zbits, ybits = nz.bit_length() - 1, ny.bit_length() - 1
    lane = lax.broadcasted_iota(jnp.int32, (ny, nz), 1)
    keep = 1.0 - 1.0 / relax_time
    everything = list(range(19))

    def wide(column):
        return jnp.broadcast_to(column, (ny, nz))

    def pack(columns):
        packed = jnp.zeros((ny, nz), jnp.float32)
        for at, (tile, edge) in enumerate(columns):
            z = nz - 1 if edge == 0 else 0
            packed = jnp.where(lane == at, wide(tile[:, z : z + 1]), packed)
        return packed

    def rim(step, edge, source, at):
        s = 0 if edge == 0 else len(zdirs) - 1
        return wide(zrecv[step, s, source, :, at : at + 1])

    loads[0].wait()
    loads[1].wait()
    f = [f_v[k] for k in range(19)]
    solid = solid_v[...] > 0

    def cells(f):
        rho, mom = moments(f)
        scale = jnp.where(solid, 0.0, rho * (1.0 / relax_time))
        kept = [jnp.where(solid, f[OPPOSITE[k]], keep * f[k]) for k in range(19)]
        return mom, 1.0 / rho, scale, kept

    mom, inv, scale, kept = cells(f)
    v = [m * inv for m in mom]
    a1s[0] = scale[1]
    for i, k in enumerate(XP):
        a1s[1 + i] = kept[k][1]
    for d in range(3):
        b1s[d] = v[d][0]
    b1s[3] = scale[0]
    for i, k in enumerate(XM):
        b1s[4 + i] = kept[k][0]
    pl.semaphore_wait(barrier, len(peers))
    first = [
        send(b1s, b1r, r_ss.at[0], r_rs.at[0], -1, 0),
        send(a1s, a1r, r_ss.at[1], r_rs.at[1], 1, 0),
    ]

    for load in loads[2:]:
        load.wait()

    def row(ref):
        return jnp.concatenate([ref[j : j + 1, :] for j in range(ref.shape[0])], axis=1)

    idx, off, mass = row(idx_v), row(off_v), row(mass_v)
    live = lax.broadcasted_iota(jnp.int32, (1, slots), 1) < counts_v[...]
    live = jnp.where(live, 1.0, 0.0).astype(jnp.float32)
    yidx = (idx >> zbits) & (ny - 1)
    key = ((idx >> (zbits + ybits)) << zbits) | (idx & (nz - 1))
    onehot_v[...] = jnp.where(
        lax.broadcasted_iota(jnp.int32, (2 * nz, slots), 0) == key, 1.0, 0.0
    ).astype(jnp.bfloat16)
    ymask = lax.broadcasted_iota(jnp.int32, (ny, slots), 0) == yidx
    near = 1.0 - off
    weight = (coupling * live) * mass
    wnear, wfar = weight * near, weight * off
    vel = [vel_v[d : d + 1, :] for d in range(3)]
    channels = [wnear * near, wnear * off, wfar * off]
    channels += [wnear * vel[d] for d in range(3)]
    channels += [wfar * vel[d] for d in range(3)]
    n_ch = len(channels)
    for c, channel in enumerate(channels):
        for h, part in enumerate(halves(channel)):
            at = (h * n_ch + c) * ny
            coef_v[at : at + ny, :] = jnp.where(ymask, part, 0.0).astype(jnp.bfloat16)
    sums = lax.dot_general(
        coef_v[...],
        onehot_v[...],
        (((1,), (1,)), ((), ())),
        preferred_element_type=jnp.float32,
    )
    sums = (sums[: n_ch * ny] + sums[n_ch * ny :]) * relax_time

    def moment(c, x):
        return sums[c * ny : (c + 1) * ny, x * nz : (x + 1) * nz]

    a, b, e = [[moment(c, x) for x in range(2)] for c in range(3)]
    part0, part1, spill = [], [], []
    for d in range(3):
        q = [moment(3 + d, x) for x in range(2)]
        r = [moment(6 + d, x) for x in range(2)]
        extra = relax_time * body_force if d == 0 else 0.0
        part0.append(q[0] - a[0] * v[d][0] - b[0] * v[d][1] + extra)
        part1.append(
            (q[1] - a[1] * v[d][1]) + (r[0] - b[0] * v[d][0] - e[0] * v[d][1]) + extra
        )
        spill.append(r[1] - b[1] * v[d][1])
    m0 = [mom[d][0] + part0[d] for d in range(3)]
    m1 = [mom[d][1] + part1[d] for d in range(3)]
    for d in range(3):
        b2s[d] = m0[d]
        a2s[d] = spill[d]
        a2s[4 + d] = m1[d]
    a2s[3] = e[1]
    a2s[7] = b[1]
    first += [
        send(a2s, a2r, r_ss.at[2], r_rs.at[2], 1, 0),
        send(b2s, b2r, r_ss.at[3], r_rs.at[3], -1, 0),
    ]
    at0, at1, columns = {}, {}, []
    for edge, ks in enumerate((ZP, ZM)):
        at0[edge] = len(columns)
        for tile in [v[d][0] for d in range(3)] + m0 + [scale[0]] + [kept[k][0] for k in ks]:
            columns.append((tile, edge))
        at1[edge] = len(columns)
        for tile in spill + [e[1]] + m1 + [b[1], scale[1]] + [kept[k][1] for k in ks]:
            columns.append((tile, edge))
    zsend[0] = pack(columns)
    first += send_rim(0)

    for copy in first:
        copy.wait_recv()
    vfront = [b1r[d] for d in range(3)]
    force = [
        jnp.stack(
            [part0[d] + (a2r[d] - a2r[3] * v[d][0]), part1[d] - b[1] * vfront[d]]
        )
        for d in range(3)
    ]

    def inverse(scale):
        return 1.0 / (relax_time * jnp.where(scale > 0.0, scale, 1.0))

    by = collide(everything, kept, [mom[d] + force[d] for d in range(3)], inv, scale)
    before = collide(
        XP,
        {k: a1r[1 + i] for i, k in enumerate(XP)},
        [a2r[4 + d] - a2r[7] * v[d][0] for d in range(3)],
        inverse(a1r[0]),
        a1r[0],
    )
    after = collide(
        XM,
        {k: b1r[4 + i] for i, k in enumerate(XM)},
        [b2r[d] + (spill[d] - e[1] * vfront[d]) for d in range(3)],
        inverse(b1r[3]),
        b1r[3],
    )
    rims = {}
    for edge, ks in enumerate((ZP, ZM)):
        flow = {s: [rim(0, edge, s, at0[edge] + d) for d in range(3)] for s in (1, 2)}
        drag = {s: [rim(0, edge, s, at1[edge] + d) for d in range(4)] for s in (0, 1)}
        for source, x in ((1, 0), (1, 1), (0, 1), (2, 0)):
            want = [k for k in ks if source == 1 or LATTICE[k][0] == 1 - source]
            if x == 0:
                at = at0[edge] + 3
                t = drag[source - 1]
                m = [
                    rim(0, edge, source, at + d) + (t[d] - t[3] * flow[source][d])
                    for d in range(3)
                ]
                at = at + 3
            else:
                at = at1[edge] + 4
                ahead = rim(0, edge, source, at + 3)
                m = [
                    rim(0, edge, source, at + d) - ahead * flow[source + 1][d]
                    for d in range(3)
                ]
                at = at + 4
            cell_scale = rim(0, edge, source, at)
            known = {k: rim(0, edge, source, at + 1 + ks.index(k)) for k in want}
            post = collide(want, known, m, inverse(cell_scale), cell_scale)
            for k in want:
                rims[k, source, x] = post[k]

    def stream(k, by, before, after, column):
        cx, cy, cz = LATTICE[k]
        if cx == 1:
            planes = [(before[k], 0, 1), (by[k][0], 1, 0)]
        elif cx == -1:
            planes = [(by[k][1], 1, 1), (after[k], 2, 0)]
        else:
            planes = [(by[k][0], 1, 0), (by[k][1], 1, 1)]
        done = []
        for plane, source, x in planes:
            if cz:
                plane = pltpu.roll(plane, 1 if cz == 1 else nz - 1, 1)
                plane = jnp.where(
                    lane == (0 if cz == 1 else nz - 1), column(k, source, x), plane
                )
            if cy:
                plane = pltpu.roll(plane, 1 if cy == 1 else ny - 1, 0)
            done.append(plane)
        return done

    f = [
        jnp.stack(stream(k, by, before, after, lambda *key: rims[key])) for k in everything
    ]

    mom, inv, scale, kept = cells(f)
    by = collide(everything, kept, [mom[d] + force[d] for d in range(3)], inv, scale)
    for i, k in enumerate(XP):
        xp_send[i] = by[k][1]
    for i, k in enumerate(XM):
        xm_send[i] = by[k][0]
    last = [
        send(xp_send, xp_recv, x_ss.at[0], x_rs.at[0], 1, 0),
        send(xm_send, xm_recv, x_ss.at[1], x_rs.at[1], -1, 0),
    ]
    zsend[1] = pack([(by[k][x], 0 if LATTICE[k][2] == 1 else 1) for k, x in LANES])
    last += send_rim(1)

    here = [jnp.concatenate([v[d][0], v[d][1]], axis=1) for d in range(3)]
    ahead = [jnp.concatenate([v[d][1], vfront[d]], axis=1) for d in range(3)]
    high, low = halves(jnp.concatenate(here + ahead, axis=0))
    oh = onehot_v[...]
    found = jnp.dot(high.astype(jnp.bfloat16), oh, preferred_element_type=jnp.float32)
    found = found + jnp.dot(low.astype(jnp.bfloat16), oh, preferred_element_type=jnp.float32)
    for d in range(3):
        mix = near * found[d * ny : (d + 1) * ny] + off * found[(3 + d) * ny : (4 + d) * ny]
        flow = jnp.sum(jnp.where(ymask, mix, 0.0), axis=0, keepdims=True)
        new = vel[d] + coupling * live * (flow - vel[d])
        if d == 1:
            new = new - settle * live
        nv_v[d : d + 1, :] = new

    def column(k, source, x):
        return rim(1, 0 if LATTICE[k][2] == 1 else 1, source, LANES[k, x])

    for copy in last:
        copy.wait_recv()
    before = {k: xp_recv[i] for i, k in enumerate(XP)}
    after = {k: xm_recv[i] for i, k in enumerate(XM)}
    for k in everything:
        for x, plane in enumerate(stream(k, by, before, after, column)):
            out_v[k, x] = plane
    for copy in sent:
        copy.wait_send()


def store(a_in, b_in, a_out, b_out, sems):
    copies = [
        pltpu.make_async_copy(a_in, a_out, sems.at[0]),
        pltpu.make_async_copy(b_in, b_out, sems.at[1]),
    ]
    for copy in copies:
        copy.start()
    for copy in copies:
        copy.wait()


def body(n_gx, n_gz, populations, solid, cell_index, offset, velocity, mass, counts):
    depth_x, ny, nz = populations.shape[1:]
    slots = cell_index.shape[0]
    rows = (slots // nz, nz)
    nzs = 1 if n_gz == 2 else 2
    f32, vmem, dma = jnp.float32, pltpu.VMEM, pltpu.SemaphoreType.DMA
    shapes = (
        jax.ShapeDtypeStruct(populations.shape, f32),
        jax.ShapeDtypeStruct(velocity.shape, f32),
    )
    held = pl.pallas_call(
        functools.partial(kernel, n_gx, n_gz),
        out_shape=shapes,
        in_specs=[pl.BlockSpec(memory_space=pltpu.HBM)] * 6
        + [pl.BlockSpec(memory_space=pl.ANY)],
        out_specs=[pl.BlockSpec(memory_space=pltpu.VMEM)] * 2,
        scratch_shapes=[
            vmem(populations.shape, f32),
            vmem(solid.shape, jnp.int32),
            vmem(rows, jnp.int32),
            vmem(rows, f32),
            vmem(velocity.shape, f32),
            vmem(rows, f32),
            vmem((1, 1), jnp.int32),
            vmem((2 * nz, slots), jnp.bfloat16),
            vmem((18 * ny, slots), jnp.bfloat16),
            *[vmem((n, ny, nz), f32) for n in (6, 6, 8, 8, 9, 9, 3, 3, 5, 5, 5, 5, 2)],
            vmem((2, nzs, 3, ny, nz), f32),
            dma((7,)),
            dma((4,)),
            dma((4,)),
            dma((2,)),
            dma((2,)),
            dma((2, nzs, 3)),
            dma((2, nzs, 3)),
        ],
        compiler_params=pltpu.CompilerParams(
            collective_id=0, has_side_effects=True, vmem_limit_bytes=32 * 1024 * 1024
        ),
    )(
        *[
            pltpu.with_memory_space_constraint(value, pltpu.HBM)
            for value in (
                populations,
                solid,
                cell_index.reshape(rows),
                offset.reshape(rows),
                velocity,
                mass.reshape(rows),
            )
        ],
        counts,
    )
    return pl.pallas_call(
        store,
        out_shape=shapes,
        in_specs=[pl.BlockSpec(memory_space=pltpu.VMEM)] * 2,
        out_specs=[pl.BlockSpec(memory_space=pltpu.HBM)] * 2,
        scratch_shapes=[dma((2,))],
        compiler_params=pltpu.CompilerParams(vmem_limit_bytes=2 * 1024 * 1024),
    )(*held)


def solution(mesh):
    return jax.shard_map(
        functools.partial(body, mesh.shape["gx"], mesh.shape["gz"]),
        mesh=mesh,
        in_specs=(
            P(None, "gx", None, "gz"),
            P("gx", None, "gz"),
            P(("gx", "gz")),
            P(("gx", "gz")),
            P(None, ("gx", "gz")),
            P(("gx", "gz")),
            P("gx", "gz"),
        ),
        out_specs=(P(None, "gx", None, "gz"), P(None, ("gx", "gz"))),
        check_vma=False,
    )
```

time: 21.7 us -> 19.2 us (0.88)
  Pallas kernels: 20.3 us -> 17.8 us
    pallas_call x1, Pallas kernels: 19.5 us -> 17 us  [body(): pl.pallas_call(functools.partial(kernel, n_gx, n_gz), out_shape=shapes, i...]
where the time goes in v3:
time: 19.2 us; the launch traced here: 19.1 us
  Pallas kernels  17.8 us (93%)
  between operations  1.29 us (7%)
    pallas_call x1, Pallas kernels, body(): pl.pallas_call(functools.partial(kernel, n_gx, n_gz), out_shape=shapes, i...  17 us
    pallas_call x1, Pallas kernels, body(): pl.pallas_call(store, out_shape=shapes, in_specs=[pl.BlockSpec(memory_spa...  0.74 us

profile of v3, /device:TPU:0, one launch (start us, length us, event | category | flops | bytes accessed | tf_op | source)
XLA Modules:
  0.0 19.1 jit_solution(5869303652739109355)
XLA Ops:
  1.3 17.0 %shard_map.86 = (f32[19,2,16,128]{3,2,1,0:T(8,128)S(1)}, f32[3,2048]{1,0:T(4,128)S(1)}) custom-call(f32[19,2,16,128]{3,2,1,0:T(8,128)} %pops_in.1, s32[2,16,128]{2,1,0:T(8,128)} %solid_in.1, s32[16,128]{1,0:T(8,128)} %bitcast.3, f32[16,128]{1,0:T(8,128)} %bitcast.4, f32[3,2048]{1,0:T(4,128)} %vel_in.1, f32[16,128]{1,0:T(8,128)} %bitcast.5, ...), custom_call_target="tpu_custom_call" | custom-call | tf_op jit(solution)/shard_map/pallas_call | solution.py:430
  18.3 0.7 %shard_map.87 = (f32[19,2,16,128]{3,2,1,0:T(8,128)}, f32[3,2048]{1,0:T(4,128)}) custom-call(f32[19,2,16,128]{3,2,1,0:T(8,128)S(1)} %get-tuple-element.4.a_in, f32[3,2048]{1,0:T(4,128)S(1)} %get-tuple-element.5.b_in), custom_call_target="tpu_custom_call" | custom-call | tf_op jit(solution)/shard_map/pallas_call | solution.py:473

commit v4 on v3

--- a/solution.py
+++ b/solution.py
@@ -175,9 +175,10 @@
     def wide(column):
         return jnp.broadcast_to(column, (ny, nz))
 
-    def pack(columns):
-        packed = jnp.zeros((ny, nz), jnp.float32)
-        for at, (tile, edge) in enumerate(columns):
+    def pack(columns, packed=None, first=0):
+        if packed is None:
+            packed = jnp.zeros((ny, nz), jnp.float32)
+        for at, (tile, edge) in enumerate(columns, first):
             z = nz - 1 if edge == 0 else 0
             packed = jnp.where(lane == at, wide(tile[:, z : z + 1]), packed)
         return packed
@@ -212,6 +213,16 @@
         send(b1s, b1r, r_ss.at[0], r_rs.at[0], -1, 0),
         send(a1s, a1r, r_ss.at[1], r_rs.at[1], 1, 0),
     ]
+
+    at0, at1, columns = {}, {}, []
+    for edge, ks in enumerate((ZP, ZM)):
+        at0[edge] = len(columns)
+        for tile in [v[d][0] for d in range(3)] + [scale[0]] + [kept[k][0] for k in ks]:
+            columns.append((tile, edge))
+        at1[edge] = len(columns)
+        for tile in [scale[1]] + [kept[k][1] for k in ks]:
+            columns.append((tile, edge))
+    packed = pack(columns)
 
     for load in loads[2:]:
         load.wait()
@@ -270,21 +281,16 @@
         a2s[4 + d] = m1[d]
     a2s[3] = e[1]
     a2s[7] = b[1]
+    late = len(columns)
+    late_columns = [
+        (tile, edge) for edge in range(2) for tile in m0 + spill + [e[1]] + m1 + [b[1]]
+    ]
+    zsend[0] = pack(late_columns, packed, late)
+    rims_in = send_rim(0)
     first += [
         send(a2s, a2r, r_ss.at[2], r_rs.at[2], 1, 0),
         send(b2s, b2r, r_ss.at[3], r_rs.at[3], -1, 0),
     ]
-    at0, at1, columns = {}, {}, []
-    for edge, ks in enumerate((ZP, ZM)):
-        at0[edge] = len(columns)
-        for tile in [v[d][0] for d in range(3)] + m0 + [scale[0]] + [kept[k][0] for k in ks]:
-            columns.append((tile, edge))
-        at1[edge] = len(columns)
-        for tile in spill + [e[1]] + m1 + [b[1], scale[1]] + [kept[k][1] for k in ks]:
-            columns.append((tile, edge))
-    zsend[0] = pack(columns)
-    first += send_rim(0)
-
     for copy in first:
         copy.wait_recv()
     vfront = [b1r[d] for d in range(3)]
@@ -314,27 +320,28 @@
         b1r[3],
     )
     rims = {}
+    for copy in rims_in:
+        copy.wait_recv()
     for edge, ks in enumerate((ZP, ZM)):
+        base = late + 11 * edge
         flow = {s: [rim(0, edge, s, at0[edge] + d) for d in range(3)] for s in (1, 2)}
-        drag = {s: [rim(0, edge, s, at1[edge] + d) for d in range(4)] for s in (0, 1)}
+        drag = {s: [rim(0, edge, s, base + 3 + d) for d in range(4)] for s in (0, 1)}
         for source, x in ((1, 0), (1, 1), (0, 1), (2, 0)):
             want = [k for k in ks if source == 1 or LATTICE[k][0] == 1 - source]
             if x == 0:
                 at = at0[edge] + 3
                 t = drag[source - 1]
                 m = [
-                    rim(0, edge, source, at + d) + (t[d] - t[3] * flow[source][d])
+                    rim(0, edge, source, base + d) + (t[d] - t[3] * flow[source][d])
                     for d in range(3)
                 ]
-                at = at + 3
             else:
-                at = at1[edge] + 4
-                ahead = rim(0, edge, source, at + 3)
+                at = at1[edge]
+                ahead = rim(0, edge, source, base + 10)
                 m = [
-                    rim(0, edge, source, at + d) - ahead * flow[source + 1][d]
+                    rim(0, edge, source, base + 7 + d) - ahead * flow[source + 1][d]
                     for d in range(3)
                 ]
-                at = at + 4
             cell_scale = rim(0, edge, source, at)
             known = {k: rim(0, edge, source, at + 1 + ks.index(k)) for k in want}
             post = collide(want, known, m, inverse(cell_scale), cell_scale)
@@ -367,6 +374,8 @@
 
     mom, inv, scale, kept = cells(f)
     by = collide(everything, kept, [mom[d] + force[d] for d in range(3)], inv, scale)
+    zsend[1] = pack([(by[k][x], 0 if LATTICE[k][2] == 1 else 1) for k, x in LANES])
+    rims_in = send_rim(1)
     for i, k in enumerate(XP):
         xp_send[i] = by[k][1]
     for i, k in enumerate(XM):
@@ -375,8 +384,6 @@
         send(xp_send, xp_recv, x_ss.at[0], x_rs.at[0], 1, 0),
         send(xm_send, xm_recv, x_ss.at[1], x_rs.at[1], -1, 0),
     ]
-    zsend[1] = pack([(by[k][x], 0 if LATTICE[k][2] == 1 else 1) for k, x in LANES])
-    last += send_rim(1)
 
     here = [jnp.concatenate([v[d][0], v[d][1]], axis=1) for d in range(3)]
     ahead = [jnp.concatenate([v[d][1], vfront[d]], axis=1) for d in range(3)]
@@ -395,13 +402,22 @@
     def column(k, source, x):
         return rim(1, 0 if LATTICE[k][2] == 1 else 1, source, LANES[k, x])
 
+    before = {k: xp_recv.at[i] for i, k in enumerate(XP)}
+    after = {k: xm_recv.at[i] for i, k in enumerate(XM)}
+
+    def write(ks):
+        for k in ks:
+            ghosts = [{k: ref[k][...]} if k in ref else {} for ref in (before, after)]
+            for x, plane in enumerate(stream(k, by, *ghosts, column)):
+                out_v[k, x] = plane
+
+    write([k for k in everything if not LATTICE[k][0] and not LATTICE[k][2]])
     for copy in last:
         copy.wait_recv()
-    before = {k: xp_recv[i] for i, k in enumerate(XP)}
-    after = {k: xm_recv[i] for i, k in enumerate(XM)}
-    for k in everything:
-        for x, plane in enumerate(stream(k, by, before, after, column)):
-            out_v[k, x] = plane
+    write([k for k in everything if LATTICE[k][0] and not LATTICE[k][2]])
+    for copy in rims_in:
+        copy.wait_recv()
+    write([k for k in everything if LATTICE[k][2]])
     for copy in sent:
         copy.wait_send()
 

time: 19.2 us -> 18.8 us (0.979)
  Pallas kernels: 17.8 us -> 17.3 us
    pallas_call x1, Pallas kernels: 17 us -> 16.6 us  [body(): pl.pallas_call(functools.partial(kernel, n_gx, n_gz), out_shape=shapes, i...]
where the time goes in v4:
time: 18.8 us; the launch traced here: 18.6 us
  Pallas kernels  17.3 us (92%)
  between operations  1.29 us (7%)
    pallas_call x1, Pallas kernels, body(): pl.pallas_call(functools.partial(kernel, n_gx, n_gz), out_shape=shapes, i...  16.6 us
    pallas_call x1, Pallas kernels, body(): pl.pallas_call(store, out_shape=shapes, in_specs=[pl.BlockSpec(memory_spa...  0.74 us

profile of v4, /device:TPU:0, one launch (start us, length us, event | category | flops | bytes accessed | tf_op | source)
XLA Modules:
  0.0 18.6 jit_solution(3926708330003159308)
XLA Ops:
  1.3 16.6 %shard_map.86 = (f32[19,2,16,128]{3,2,1,0:T(8,128)S(1)}, f32[3,2048]{1,0:T(4,128)S(1)}) custom-call(f32[19,2,16,128]{3,2,1,0:T(8,128)} %pops_in.1, s32[2,16,128]{2,1,0:T(8,128)} %solid_in.1, s32[16,128]{1,0:T(8,128)} %bitcast.3, f32[16,128]{1,0:T(8,128)} %bitcast.4, f32[3,2048]{1,0:T(4,128)} %vel_in.1, f32[16,128]{1,0:T(8,128)} %bitcast.5, ...), custom_call_target="tpu_custom_call" | custom-call | tf_op jit(solution)/shard_map/pallas_call | solution.py:446
  17.9 0.7 %shard_map.87 = (f32[19,2,16,128]{3,2,1,0:T(8,128)}, f32[3,2048]{1,0:T(4,128)}) custom-call(f32[19,2,16,128]{3,2,1,0:T(8,128)S(1)} %get-tuple-element.4.a_in, f32[3,2048]{1,0:T(4,128)S(1)} %get-tuple-element.5.b_in), custom_call_target="tpu_custom_call" | custom-call | tf_op jit(solution)/shard_map/pallas_call | solution.py:489
